TPU v7x, 128 devices: a whole 4x4x4 slice. The times are simulated.
128 devices in a mesh: section: 2 (over core), seq: 8 (over y, x_lo), mp: 8 (over x_hi, z).
Axes of the slice: x: 4 (x_hi: 2, x_lo: 2; x = x_hi * 2 + x_lo), y: 4, z: 4, core: 2. Of those that a mesh axis runs over, the one named last changes fastest.
Arguments:
- bottleneck: bfloat16 [2, 1024, 4096], P('section', ('seq', 'mp')), may hold values from -6 to 6
- qkv_weight: bfloat16 [3, 4096, 4096], P(None, None, ('section', 'mp')), may hold values from -0.2 to 0.2
- out_weight: bfloat16 [4096, 4096], P(('section', 'mp')), may hold values from -0.5 to 0.5
- up_weight: bfloat16 [4096, 16384], P(None, ('section', 'mp')), may hold values from -0.09375 to 0.09375
- down_weight: bfloat16 [16384, 4096], P(('section', 'mp')), may hold values from -0.046875 to 0.046875
- cotangent: bfloat16 [2, 1024, 4096], P('section', ('seq', 'mp')), may hold values from -6 to 6
Outputs:
- block_out: bfloat16 [2, 1024, 4096], P('section', ('seq', 'mp'))
- grad_input: bfloat16 [2, 1024, 4096], P('section', ('seq', 'mp'))
All inputs are finite; a program needn't handle non-finite values.
Results may differ from a plain program's by a relative error of at most 0.025.
Values may be sent and summed in bfloat16 or wider, within the bound.
No kernel may reach another device: no remote copies, remote signals or barrier semaphores. Data moves between devices by JAX's collectives and lax.ppermute only.
A program may use at most 128 MiB of HBM per device.

v0:
```python
import math
import jax
import jax.numpy as jnp
from jax import lax
from jax.sharding import PartitionSpec as P

HD = 128
norm_eps = 1e-06


def layer_norm(inputs):
    row_mean = jnp.mean(inputs, axis=-1, keepdims=True)
    centered = inputs - row_mean
    inv_std = lax.rsqrt(jnp.mean(centered * centered, axis=-1, keepdims=True) + norm_eps)
    return (centered * inv_std, inv_std)


def norm_backward(normed, inv_std, grad_in):
    mean_grad = jnp.mean(grad_in, axis=-1, keepdims=True)
    mean_mix = jnp.mean(grad_in * normed, axis=-1, keepdims=True)
    return inv_std * (grad_in - mean_grad - normed * mean_mix)


def gelu_value(pre_act):
    return pre_act * 0.5 * (1.0 + lax.erf(pre_act * 0.7071067811865476))


def gelu_slope(pre_act):
    cumul = 0.5 * (1.0 + lax.erf(pre_act * 0.7071067811865476))
    return cumul + pre_act * jnp.exp(-0.5 * pre_act * pre_act) * 0.3989422804014327


def swap_section(data):
    return lax.ppermute(data, "section", [(0, 1), (1, 0)])


def spread(own, axis):
    size = lax.axis_size(axis)
    copies = jnp.broadcast_to(own[None], (size,) + own.shape)
    return lax.all_to_all(copies, axis, 0, 0)


def gather_rows(own):
    mine = spread(own, "mp").reshape(-1, own.shape[-1])
    return jnp.concatenate([mine, swap_section(mine)], axis=0)


def scatter_rows(partial):
    half = partial.shape[0] // 2
    width = partial.shape[1]
    other = swap_section(partial[half:].astype(jnp.bfloat16))
    pair = (partial[:half] + other.astype(jnp.float32)).astype(jnp.bfloat16)
    size = lax.axis_size("mp")
    parts = lax.all_to_all(pair.reshape(size, half // size, width), "mp", 0, 0)
    return jnp.sum(parts.astype(jnp.float32), axis=0)


def scatter_rows_later(partial):
    half = partial.shape[0] // 2
    other = swap_section(partial[half:].astype(jnp.bfloat16))
    pair = (partial[:half] + other.astype(jnp.float32)).astype(jnp.bfloat16)
    return lax.psum_scatter(pair, "mp", scatter_dimension=0, tiled=True).astype(jnp.float32)


def gather_rows_early(own):
    mine = lax.all_gather(own, "mp", axis=0, tiled=True)
    return jnp.concatenate([mine, swap_section(mine)], axis=0)


def dot_f32(lhs, rhs):
    return jnp.dot(lhs, rhs, preferred_element_type=jnp.float32)


def dot_nt(lhs, rhs):
    return jnp.einsum("tf,df->td", lhs, rhs, preferred_element_type=jnp.float32)


def per_device(bottleneck, qkv_weight, out_weight, up_weight, down_weight, cotangent):
    own_in = bottleneck[0].astype(jnp.float32)
    own_cot = cotangent[0]
    images = 2
    head_cols = qkv_weight.shape[2]
    head_count = head_cols // HD
    score_scale = 1.0 / math.sqrt(HD)
    cot_all = gather_rows_early(own_cot)
    normed_one, inv_one = layer_norm(own_in)
    normed_all = gather_rows(normed_one.astype(jnp.bfloat16))
    total_rows = normed_all.shape[0]
    block_rows = total_rows // images
    projected = jnp.einsum(
        "td,kdf->ktf", normed_all, qkv_weight, preferred_element_type=jnp.float32
    ).astype(jnp.bfloat16)
    query_heads = projected[0].reshape(images, block_rows, head_count, HD)
    pairs = spread(projected[1:].reshape(2, images, block_rows, head_cols), "seq")
    seq_size = pairs.shape[0]
    length = seq_size * block_rows
    heads = jnp.transpose(pairs, (1, 2, 0, 3, 4)).reshape(2, images, length, head_count, HD)
    key_heads, value_heads = (heads[0], heads[1])
    scores = (
        jnp.einsum("ilhd,imhd->ihlm", query_heads, key_heads, preferred_element_type=jnp.float32)
        * score_scale
    )
    row_max = jnp.max(scores, axis=-1)
    weights = jnp.exp(scores - row_max[..., None])
    totals = jnp.sum(weights, axis=-1)
    log_total = row_max + jnp.log(totals)
    mixed_values = jnp.einsum(
        "ihlm,imhd->ilhd",
        weights.astype(jnp.bfloat16),
        value_heads,
        preferred_element_type=jnp.float32,
    )
    attended = (mixed_values / jnp.transpose(totals, (0, 2, 1))[..., None]).astype(jnp.bfloat16)
    attn_own = scatter_rows(dot_f32(attended.reshape(total_rows, head_cols), out_weight))
    resid = (own_in + attn_own).astype(jnp.bfloat16)
    normed_two, inv_two = layer_norm(resid.astype(jnp.float32))
    normed_two_all = gather_rows(normed_two.astype(jnp.bfloat16))
    hidden_pre = dot_f32(normed_two_all, up_weight)
    hidden = gelu_value(hidden_pre).astype(jnp.bfloat16)
    grad_act = dot_nt(cot_all, down_weight)
    grad_hidden = (grad_act * gelu_slope(hidden_pre)).astype(jnp.bfloat16)
    grad_norm_two = scatter_rows(dot_nt(grad_hidden, up_weight))
    ffn_own = scatter_rows_later(dot_f32(hidden, down_weight))
    block_out = (resid.astype(jnp.float32) + ffn_own).astype(jnp.bfloat16)
    grad_resid = (
        own_cot.astype(jnp.float32) + norm_backward(normed_two, inv_two, grad_norm_two)
    ).astype(jnp.bfloat16)
    grad_resid_all = gather_rows(grad_resid)
    grad_attn = dot_nt(grad_resid_all, out_weight).astype(jnp.bfloat16)
    grad_attn_heads = grad_attn.reshape(images, block_rows, head_count, HD)
    row_delta = jnp.sum(grad_attn_heads.astype(jnp.float32) * attended.astype(jnp.float32), axis=-1)
    prob_rows = jnp.exp(scores - log_total[..., None])
    grad_probs = jnp.einsum(
        "ilhd,imhd->ihlm", grad_attn_heads, value_heads, preferred_element_type=jnp.float32
    )
    grad_scores = (
        prob_rows * (grad_probs - jnp.transpose(row_delta, (0, 2, 1))[..., None]) * score_scale
    ).astype(jnp.bfloat16)
    grad_query = jnp.einsum(
        "ihlm,imhd->ilhd", grad_scores, key_heads, preferred_element_type=jnp.float32
    ).astype(jnp.bfloat16)
    key_terms = jnp.einsum(
        "ihlm,ilhd->imhd", grad_scores, query_heads, preferred_element_type=jnp.float32
    ).astype(jnp.bfloat16)
    value_terms = jnp.einsum(
        "ihlm,ilhd->imhd",
        prob_rows.astype(jnp.bfloat16),
        grad_attn_heads,
        preferred_element_type=jnp.float32,
    ).astype(jnp.bfloat16)
    terms = jnp.stack([key_terms, value_terms]).reshape(2, images, seq_size, block_rows, head_cols)
    terms = lax.all_to_all(jnp.transpose(terms, (2, 0, 1, 3, 4)), "seq", 0, 0)
    grad_kv = jnp.sum(terms.astype(jnp.float32), axis=0).astype(jnp.bfloat16)
    grad_qkv = jnp.concatenate(
        [grad_query.reshape(1, total_rows, head_cols), grad_kv.reshape(2, total_rows, head_cols)]
    )
    grad_norm_one = scatter_rows(
        jnp.einsum("ktf,kdf->td", grad_qkv, qkv_weight, preferred_element_type=jnp.float32)
    )
    grad_input = (
        grad_resid.astype(jnp.float32) + norm_backward(normed_one, inv_one, grad_norm_one)
    ).astype(jnp.bfloat16)
    return (block_out[None], grad_input[None])


def solution(mesh):
    in_specs = (
        P("section", ("seq", "mp"), None),
        P(None, None, ("section", "mp")),
        P(("section", "mp"), None),
        P(None, ("section", "mp")),
        P(("section", "mp"), None),
        P("section", ("seq", "mp"), None),
    )
    out_specs = (P("section", ("seq", "mp"), None), P("section", ("seq", "mp"), None))
    return jax.shard_map(
        per_device, mesh=mesh, in_specs=in_specs, out_specs=out_specs, check_vma=False
    )
```

profile of v0, /device:TPU:0, one launch (start us, length us, event | category | flops | bytes accessed | tf_op | source)
XLA Modules:
  0.0 379.1 jit_solution(5679118020968333429)
XLA Ops:
  7.2 1.2 convert_reduce_fusion.5
  8.4 1.1 fusion.64
  9.5 1.0 fusion.83
  10.6 24.8 %all_to_all.40 = bf16[8,16,4096]{2,1,0:T(8,128)(2,1)S(1)} all-to-all(bf16[8,16,4096]{2,1,0:T(8,128)(2,1)S(1)} %broadcast_in_dim.19), channel_id=1, replica_groups=mesh['section'=2,'seq'=8,'mp'=8] {'mp'}, dimensions={0} | all-to-all | bytes 2097152 | tf_op jit(solution)/shard_map/all_to_all | solution.py:40
  35.4 2.7 collective-permute-done
  38.1 4.6 %fusion.29 = bf16[3,256,256]{2,1,0:T(8,128)(2,1)S(1)} fusion(bf16[3,4096,256]{2,1,0:T(8,128)(2,1)} %param.7, bf16[128,4096]{1,0:T(8,128)(2,1)S(1)} %collective-permute-done, bf16[128,4096]{1,0:T(8,128)(2,1)S(1)} %bitcast.138), kind=kOutput, calls=%fused_computation.48 | convolution fusion | flops 1615003648 | bytes 8781824 | tf_op jit(solution)/shard_map/td,kdf->ktf/dot_general | solution.py:90
  42.9 1.8 broadcast_in_dim.21
  44.7 4.6 %all-to-all-start.1 = ((bf16[8,2,2,128,256]{3,4,2,1,0:T(8,128)(2,1)}), bf16[8,2,2,128,256]{3,4,2,1,0:T(8,128)(2,1)}, u32[]{:S(2)}, u32[]{:S(2)}) async-start(bf16[8,2,2,128,256]{3,4,2,1,0:T(8,128)(2,1)} %broadcast_in_dim.21), calls=%async_computation.1 | async-start | bytes 4194304 | tf_op jit(solution)/shard_map/all_to_all | solution.py:40
  49.5 27.2 %all-to-all-done.1 = bf16[8,2,2,128,256]{3,4,2,1,0:T(8,128)(2,1)} async-done(((bf16[8,2,2,128,256]{3,4,2,1,0:T(8,128)(2,1)}), bf16[8,2,2,128,256]{3,4,2,1,0:T(8,128)(2,1)}, u32[]{:S(2)}, u32[]{:S(2)}) %all-to-all-start.1) | async-done | bytes 2097184 | tf_op jit(solution)/shard_map/all_to_all | solution.py:40
  76.6 2.7 fusion.99
  79.3 1.7 copy.26
  81.0 1.5 squeeze.11
  82.5 3.3 copy.25
  85.8 2.3 squeeze.10
  89.2 0.9 copy-done.1
  90.8 0.7 fusion.85
  91.8 2.6 collective-permute-done.1
  94.6 20.7 %all_to_all.41 = bf16[8,16,4096]{2,1,0:T(8,128)(2,1)S(1)} all-to-all(bf16[8,16,4096]{2,1,0:T(8,128)(2,1)S(1)} %bitcast.130), channel_id=1, replica_groups=mesh['section'=2,'seq'=8,'mp'=8] {'mp'}, dimensions={0} | all-to-all | bytes 2097152 | tf_op jit(solution)/shard_map/all_to_all | solution.py:54
  116.0 1.1 broadcast_in_dim.23
  117.1 4.2 %all-to-all-start.3 = ((bf16[8,16,4096]{2,1,0:T(8,128)(2,1)}), bf16[8,16,4096]{2,1,0:T(8,128)(2,1)}, u32[]{:S(2)}, u32[]{:S(2)}) async-start(bf16[8,16,4096]{2,1,0:T(8,128)(2,1)} %broadcast_in_dim.23), calls=%async_computation.3 | async-start | bytes 2097152 | tf_op jit(solution)/shard_map/all_to_all | solution.py:40
  122.1 13.8 %all-to-all-done.3 = bf16[8,16,4096]{2,1,0:T(8,128)(2,1)} async-done(((bf16[8,16,4096]{2,1,0:T(8,128)(2,1)}), bf16[8,16,4096]{2,1,0:T(8,128)(2,1)}, u32[]{:S(2)}, u32[]{:S(2)}) %all-to-all-start.3) | async-done | bytes 1048608 | tf_op jit(solution)/shard_map/all_to_all | solution.py:40
  135.9 35.0 %all-gather.3.cloned.1.call-done = bf16[1,128,4096]{2,1,0:T(8,128)(2,1)} async-done(((bf16[1,16,4096]{2,1,0:T(8,128)(2,1)}), bf16[1,128,4096]{2,1,0:T(8,128)(2,1)}) %all-gather.3.cloned.1.call-update) | async-done | bytes 1048592 | tf_op jit(solution)/shard_map/all_gather | solution.py:66
  170.9 6.5 %fusion.7 = f32[256,1024]{1,0:T(8,128)S(1)} fusion(bf16[4096,1024]{1,0:T(8,128)(2,1)} %param.9, bf16[128,4096]{1,0:T(8,128)(2,1)} %collective-permute-done.2, bf16[128,4096]{1,0:T(8,128)(2,1)} %bitcast.12), kind=kOutput, calls=%fused_computation.21 | convolution fusion | flops 2151677952 | bytes 11534336 | tf_op jit(solution)/shard_map/dot_general | solution.py:71
  177.5 2.3 fusion.47
  179.9 2.0 copy-done.6
  181.8 1.1 slice.84
  182.9 0.9 collective-permute-start.3
  183.9 13.4 %fusion.45 = f32[256,4096]{1,0:T(8,128)} fusion(bf16[4096,1024]{1,0:T(8,128)(2,1)} %param.9, bf16[1024,4096]{1,0:T(8,128)(2,1)} %param.10, bf16[128,4096]{1,0:T(8,128)(2,1)} %collective-permute-done.4, bf16[128,4096]{1,0:T(8,128)(2,1)} %bitcast.146, f32[256,1024]{1,0:T(8,128)} %copy-done.10), kind=kOutput, calls=%fused_computation.63 | convolution fusion | flops 4301783040 | bytes 24117248 | tf_op jit(solution)/shard_map/tf,df->td/dot_general | solution.py:75
  197.3 2.7 slice.83
  200.0 3.1 fusion.2
  203.1 2.1 fusion.1
  205.2 22.3 %all_to_all.42 = bf16[8,16,4096]{2,1,0:T(8,128)(2,1)S(1)} all-to-all(bf16[8,16,4096]{2,1,0:T(8,128)(2,1)S(1)} %bitcast.131), channel_id=1, replica_groups=mesh['section'=2,'seq'=8,'mp'=8] {'mp'}, dimensions={0} | all-to-all | bytes 2097152 | tf_op jit(solution)/shard_map/all_to_all | solution.py:54
  227.9 48.2 %reduce-scatter.2.cloned.1.call-done = bf16[16,4096]{1,0:T(8,128)(2,1)} async-done(((bf16[128,4096]{1,0:T(8,128)(2,1)}), bf16[16,4096]{1,0:T(8,128)(2,1)}) %reduce-scatter.2.cloned.1.call-update) | async-done | bytes 131088 | tf_op jit(solution)/shard_map/reduce_scatter | solution.py:62
  276.1 1.7 fusion.63
  278.1 19.8 %all_to_all.43 = bf16[8,16,4096]{2,1,0:T(8,128)(2,1)S(1)} all-to-all(bf16[8,16,4096]{2,1,0:T(8,128)(2,1)S(1)} %broadcast_in_dim.26), channel_id=1, replica_groups=mesh['section'=2,'seq'=8,'mp'=8] {'mp'}, dimensions={0} | all-to-all | bytes 2097152 | tf_op jit(solution)/shard_map/all_to_all | solution.py:40
  297.9 2.6 collective-permute-done.6
  300.5 0.7 fusion.32
  301.5 2.3 convolution_convert_fusion
  303.8 2.0 multiply_convert_fusion
  307.2 1.5 maximum_bitcast_fusion.2
  308.7 4.3 %all-to-all-start.6 = ((bf16[8,2,2,128,256]{3,4,2,1,0:T(8,128)(2,1)}), bf16[8,2,2,128,256]{3,4,2,1,0:T(8,128)(2,1)}, u32[]{:S(2)}, u32[]{:S(2)}) async-start(bf16[8,2,2,128,256]{3,4,2,1,0:T(8,128)(2,1)} %maximum_bitcast_fusion.2), calls=%async_computation.7 | async-start | bytes 4194304 | tf_op jit(solution)/shard_map/all_to_all | solution.py:152
  313.1 1.7 fusion.35
  315.0 25.7 %all-to-all-done.6 = bf16[8,2,2,128,256]{3,4,2,1,0:T(8,128)(2,1)} async-done(((bf16[8,2,2,128,256]{3,4,2,1,0:T(8,128)(2,1)}), bf16[8,2,2,128,256]{3,4,2,1,0:T(8,128)(2,1)}, u32[]{:S(2)}, u32[]{:S(2)}) %all-to-all-start.6) | async-done | bytes 2097184 | tf_op jit(solution)/shard_map/all_to_all | solution.py:152
  340.6 1.9 reduce_sum.147
  342.7 4.6 %convolution_bitcast_fusion = f32[256,4096]{1,0:T(8,128)S(1)} fusion(bf16[3,4096,256]{2,1,0:T(8,128)(2,1)} %param.7, bf16[2,256,256]{2,1,0:T(8,128)(2,1)S(1)} %bitcast.134, bf16[1,256,256]{2,1,0:T(8,128)(2,1)S(1)} %reshape.277), kind=kOutput, calls=%fused_computation | convolution fusion | flops 1610809344 | bytes 10878976 | tf_op jit(solution)/shard_map/ktf,kdf->td/dot_general | solution.py:158
  347.6 2.6 collective-permute-done.7
  350.4 20.3 %all_to_all.44 = bf16[8,16,4096]{2,1,0:T(8,128)(2,1)S(1)} all-to-all(bf16[8,16,4096]{2,1,0:T(8,128)(2,1)S(1)} %bitcast.132), channel_id=1, replica_groups=mesh['section'=2,'seq'=8,'mp'=8] {'mp'}, dimensions={0} | all-to-all | bytes 2097152 | tf_op jit(solution)/shard_map/all_to_all | solution.py:54
  371.4 0.8 fusion.75
  (82 shorter events, 8.0 us)
Async XLA Ops:
  7.2 83.7 %copy-start = (bf16[256,4096]{1,0:T(8,128)(2,1)S(1)}, bf16[256,4096]{1,0:T(8,128)(2,1)}, u32[]{:S(2)}) copy-start(bf16[256,4096]{1,0:T(8,128)(2,1)} %param.8) | copy-start | bytes 6291460
  35.4 2.7 collective-permute-start
  44.7 32.0 %all-to-all-start.1 = ((bf16[8,2,2,128,256]{3,4,2,1,0:T(8,128)(2,1)}), bf16[8,2,2,128,256]{3,4,2,1,0:T(8,128)(2,1)}, u32[]{:S(2)}, u32[]{:S(2)}) async-start(bf16[8,2,2,128,256]{3,4,2,1,0:T(8,128)(2,1)} %broadcast_in_dim.21), calls=%async_computation.1 | async-start | bytes 4194304 | tf_op jit(solution)/shard_map/all_to_all | solution.py:40
  49.4 38.7 %copy-start.7 = (bf16[2,128,2,128]{1,3,2,0:T(8,128)(2,1)}, bf16[2,128,2,128]{1,3,2,0:T(8,128)(2,1)S(1)}, u32[]{:S(2)}) copy-start(bf16[2,128,2,128]{1,3,2,0:T(8,128)(2,1)S(1)} %copy.34) | copy-start | bytes 393220
  82.5 5.6 %copy-start.3 = (bf16[2,1024,2,128]{1,3,2,0:T(8,128)(2,1)}, bf16[2,1024,2,128]{1,3,2,0:T(8,128)(2,1)S(1)}, u32[]{:S(2)}) copy-start(bf16[2,1024,2,128]{1,3,2,0:T(8,128)(2,1)S(1)} %squeeze.11) | copy-start | bytes 3145732
  88.1 2.0 copy-start.5
  88.7 1.4 copy-start.1
  91.7 2.7 collective-permute-start.1
  94.6 20.8 %copy-start.4 = (bf16[1,16,4096]{2,1,0:T(8,128)(2,1)S(1)}, bf16[1,16,4096]{2,1,0:T(8,128)(2,1)}, u32[]{:S(2)}) copy-start(bf16[1,16,4096]{2,1,0:T(8,128)(2,1)} %param.6) | copy-start | bytes 393220
  117.1 18.8 %all-to-all-start.3 = ((bf16[8,16,4096]{2,1,0:T(8,128)(2,1)}), bf16[8,16,4096]{2,1,0:T(8,128)(2,1)}, u32[]{:S(2)}, u32[]{:S(2)}) async-start(bf16[8,16,4096]{2,1,0:T(8,128)(2,1)} %broadcast_in_dim.23), calls=%async_computation.3 | async-start | bytes 2097152 | tf_op jit(solution)/shard_map/all_to_all | solution.py:40
  121.3 49.6 %all-gather.3.cloned.1.call-start = ((), (), s32[]{:S(2)}) async-start(), calls=%async_computation.10 | async-start | bytes 1179648 | tf_op jit(solution)/shard_map/all_gather | solution.py:66
  122.1 154.0 %reduce-scatter.2.cloned.1.call-start = ((), (), s32[]{:S(2)}) async-start(), calls=%async_computation.9 | async-start | bytes 1179648 | tf_op jit(solution)/shard_map/reduce_scatter | solution.py:62
  135.9 35.1 %collective-permute-start.2 = (bf16[128,4096]{1,0:T(8,128)(2,1)}, bf16[128,4096]{1,0:T(8,128)(2,1)}, u32[]{:S(2)}, u32[]{:S(2)}) collective-permute-start(bf16[128,4096]{1,0:T(8,128)(2,1)} %bitcast.12), channel_id=1, source_target_pairs={{0,64},{64,0},{1,65},{65,1},{2,66},{66,2},{3,67},{67,3},{4,68},{68... | collective-permute-start | bytes 3145736 | tf_op jit(solution)/shard_map/ppermute | solution.py:34
  170.9 6.5 %slice-start = ((s8[8388608]{0:T(1024)(128)(4,1)}), s8[4194304]{0:T(1024)(128)(4,1)S(1)}, s32[]{:S(2)}) async-start(s8[8388608]{0:T(1024)(128)(4,1)} %bitcast.143), calls=%async_computation.11 | async-start | bytes 8388608
  170.9 6.5 %slice-start.1 = ((s8[8388608]{0:T(1024)(128)(4,1)}), s8[4194304]{0:T(1024)(128)(4,1)S(1)}, s32[]{:S(2)}) async-start(s8[8388608]{0:T(1024)(128)(4,1)} %bitcast.143), calls=%async_computation.12 | async-start | bytes 8388608
  170.9 12.9 %collective-permute-start.4 = (bf16[128,4096]{1,0:T(8,128)(2,1)}, bf16[128,4096]{1,0:T(8,128)(2,1)}, u32[]{:S(2)}, u32[]{:S(2)}) collective-permute-start(bf16[128,4096]{1,0:T(8,128)(2,1)} %bitcast.145), channel_id=1, source_target_pairs={{0,64},{64,0},{1,65},{65,1},{2,66},{66,2},{3,67},{67,3},{4,68},{68... | collective-permute-start | bytes 3145736 | tf_op jit(solution)/shard_map/ppermute | solution.py:34
  177.5 2.4 copy-start.10
  179.8 2.0 copy-start.6
  182.9 17.1 %collective-permute-start.3 = (bf16[128,4096]{1,0:T(8,128)(2,1)}, bf16[128,4096]{1,0:T(8,128)(2,1)}, u32[]{:S(2)}, u32[]{:S(2)}) collective-permute-start(bf16[128,4096]{1,0:T(8,128)(2,1)} %slice.84), channel_id=1, source_target_pairs={{0,64},{64,0},{1,65},{65,1},{2,66},{66,2},{3,67},{67,3},{4,68},{68... | collective-permute-start | bytes 3145736 | tf_op jit(solution)/shard_map/ppermute | solution.py:34
  200.0 3.1 collective-permute-start.5
  205.2 72.7 %copy-start.9 = (bf16[1,16,4096]{2,1,0:T(8,128)(2,1)S(1)}, bf16[1,16,4096]{2,1,0:T(8,128)(2,1)}, u32[]{:S(2)}) copy-start(bf16[1,16,4096]{2,1,0:T(8,128)(2,1)} %param.11) | copy-start | bytes 393220
  297.9 2.7 collective-permute-start.6
  301.4 2.3 copy-start.2
  303.8 2.0 copy-start.8
  308.7 31.9 %all-to-all-start.6 = ((bf16[8,2,2,128,256]{3,4,2,1,0:T(8,128)(2,1)}), bf16[8,2,2,128,256]{3,4,2,1,0:T(8,128)(2,1)}, u32[]{:S(2)}, u32[]{:S(2)}) async-start(bf16[8,2,2,128,256]{3,4,2,1,0:T(8,128)(2,1)} %maximum_bitcast_fusion.2), calls=%async_computation.7 | async-start | bytes 4194304 | tf_op jit(solution)/shard_map/all_to_all | solution.py:152
  347.5 2.7 collective-permute-start.7
Sparse Core Ops, SparseCore 0:
  124.5 46.3 all-gather.2
  203.2 72.8 reduce-scatter.1
where the time goes:
time: 380 us; the launch traced here: 379 us
  waiting for transfers between devices  161 us (42%)
  blocking collectives  108 us (28%)
  matrix products  40.4 us (11%)
  local copies, waits for them, and re-layouts  23.5 us (6%)
  other arithmetic  17.3 us (5%)
  between operations  14.5 us (4%)
  starting transfers between devices  14.4 us (4%)
    all_to_all x3, blocking collectives, scatter_rows(): parts = lax.all_to_all(pair.reshape(size, half // size, width), 'mp', 0, 0)  63.3 us
    reduce_scatter x1, waiting for transfers between devices, scatter_rows_later(): lax.psum_scatter(pair, 'mp', scatter_dimension=0, tiled=True)  48.2 us
    all_to_all x2, blocking collectives, spread(): return lax.all_to_all(copies, axis, 0, 0)  44.6 us
    all_to_all x2, waiting for transfers between devices, spread(): return lax.all_to_all(copies, axis, 0, 0)  41 us
    all_gather x1, waiting for transfers between devices, gather_rows_early(): mine = lax.all_gather(own, 'mp', axis=0, tiled=True)  35 us
    all_to_all x1, waiting for transfers between devices, per_device(): terms = lax.all_to_all(jnp.transpose(terms, (2, 0, 1, 3, 4)), 'seq', 0, 0)  25.7 us
    dot_general x2, matrix products, dot_nt(): return jnp.einsum('tf,df->td', lhs, rhs, preferred_element_type=jnp.float32)  14.2 us
    ppermute x8, waiting for transfers between devices, swap_section(): return lax.ppermute(data, 'section', [(0, 1), (1, 0)])  10.6 us
  transfers between devices with their start and end apart: 13, of which 9 were waited for; matrix products, arithmetic and copies ran while one was open for 9% of the time, Pallas kernels for 0%

commit v1 on v0

--- a/solution.py
+++ b/solution.py
@@ -63,7 +63,9 @@
 
 
 def gather_rows_early(own):
-    mine = lax.all_gather(own, "mp", axis=0, tiled=True)
+    mine = jnp.concatenate(
+        lax.all_to_all(jnp.stack([own] * lax.axis_size("mp")), "mp", 0, 0), axis=0
+    )
     return jnp.concatenate([mine, swap_section(mine)], axis=0)
 
 

time: 380 us -> 362 us (0.953)
  waiting for transfers between devices: 161 us -> 110 us
  blocking collectives: 108 us -> 146 us
  starting transfers between devices: 14.4 us -> 9.97 us
    all_gather x1 -> x0, waiting for transfers between devices: 35 us -> none  [gather_rows_early(): mine = lax.all_gather(own, 'mp', axis=0, tiled=True)]
    all_to_all x0 -> x1, blocking collectives: none -> 20.3 us  [gather_rows_early(): lax.all_to_all(jnp.stack([own] * lax.axis_size('mp')), 'mp', 0, 0)]
    all_to_all x2 -> x3, blocking collectives: 44.6 us -> 63.9 us  [spread(): return lax.all_to_all(copies, axis, 0, 0)]
    all_to_all x2 -> x1, waiting for transfers between devices: 41 us -> 27.1 us  [spread(): return lax.all_to_all(copies, axis, 0, 0)]
    all_to_all x2 -> x1, starting transfers between devices: 8.84 us -> 4.59 us  [spread(): return lax.all_to_all(copies, axis, 0, 0)]
  transfers between devices with their start and end apart: 13 -> 11, of which waited for: 9 -> 7; matrix products, arithmetic and copies ran while one was open for 9% -> 9% of each run, Pallas kernels for 0% -> 0%
where the time goes in v1:
time: 362 us; the launch traced here: 361 us
  blocking collectives  146 us (40%)
  waiting for transfers between devices  110 us (30%)
  matrix products  40 us (11%)
  local copies, waits for them, and re-layouts  22.6 us (6%)
  other arithmetic  17.3 us (5%)
  between operations  14.5 us (4%)
  starting transfers between devices  9.97 us (3%)
    all_to_all x3, blocking collectives, spread(): return lax.all_to_all(copies, axis, 0, 0)  63.9 us
    all_to_all x3, blocking collectives, scatter_rows(): parts = lax.all_to_all(pair.reshape(size, half // size, width), 'mp', 0, 0)  62.1 us
    reduce_scatter x1, waiting for transfers between devices, scatter_rows_later(): lax.psum_scatter(pair, 'mp', scatter_dimension=0, tiled=True)  47 us
    all_to_all x1, waiting for transfers between devices, spread(): return lax.all_to_all(copies, axis, 0, 0)  27.1 us
    all_to_all x1, waiting for transfers between devices, per_device(): terms = lax.all_to_all(jnp.transpose(terms, (2, 0, 1, 3, 4)), 'seq', 0, 0)  25.7 us
    all_to_all x1, blocking collectives, gather_rows_early(): lax.all_to_all(jnp.stack([own] * lax.axis_size('mp')), 'mp', 0, 0)  20.3 us
    dot_general x2, matrix products, dot_nt(): return jnp.einsum('tf,df->td', lhs, rhs, preferred_element_type=jnp.float32)  14.2 us
    ppermute x8, waiting for transfers between devices, swap_section(): return lax.ppermute(data, 'section', [(0, 1), (1, 0)])  10.6 us
  transfers between devices with their start and end apart: 11, of which 7 were waited for; matrix products, arithmetic and copies ran while one was open for 9% of the time, Pallas kernels for 0%

profile of v1, /device:TPU:0, one launch (start us, length us, event | category | flops | bytes accessed | tf_op | source)
XLA Modules:
  0.0 361.2 jit_solution(333533420874266894)
XLA Ops:
  7.2 1.2 convert_reduce_fusion.5
  8.4 1.1 fusion.64
  9.5 1.0 fusion.83
  10.6 24.8 %all_to_all.45 = bf16[8,16,4096]{2,1,0:T(8,128)(2,1)S(1)} all-to-all(bf16[8,16,4096]{2,1,0:T(8,128)(2,1)S(1)} %broadcast_in_dim.19), channel_id=1, replica_groups=mesh['section'=2,'seq'=8,'mp'=8] {'mp'}, dimensions={0} | all-to-all | bytes 2097152 | tf_op jit(solution)/shard_map/all_to_all | solution.py:40
  35.4 2.7 collective-permute-done
  38.1 4.6 %fusion.29 = bf16[3,256,256]{2,1,0:T(8,128)(2,1)S(1)} fusion(bf16[3,4096,256]{2,1,0:T(8,128)(2,1)} %param.7, bf16[128,4096]{1,0:T(8,128)(2,1)S(1)} %collective-permute-done, bf16[128,4096]{1,0:T(8,128)(2,1)S(1)} %bitcast.143), kind=kOutput, calls=%fused_computation.48 | convolution fusion | flops 1615003648 | bytes 8781824 | tf_op jit(solution)/shard_map/td,kdf->ktf/dot_general | solution.py:92
  42.9 1.8 broadcast_in_dim.21
  44.7 4.6 %all-to-all-start.1 = ((bf16[8,2,2,128,256]{3,4,2,1,0:T(8,128)(2,1)}), bf16[8,2,2,128,256]{3,4,2,1,0:T(8,128)(2,1)}, u32[]{:S(2)}, u32[]{:S(2)}) async-start(bf16[8,2,2,128,256]{3,4,2,1,0:T(8,128)(2,1)} %broadcast_in_dim.21), calls=%async_computation.1 | async-start | bytes 4194304 | tf_op jit(solution)/shard_map/all_to_all | solution.py:40
  49.5 27.1 %all-to-all-done.1 = bf16[8,2,2,128,256]{3,4,2,1,0:T(8,128)(2,1)} async-done(((bf16[8,2,2,128,256]{3,4,2,1,0:T(8,128)(2,1)}), bf16[8,2,2,128,256]{3,4,2,1,0:T(8,128)(2,1)}, u32[]{:S(2)}, u32[]{:S(2)}) %all-to-all-start.1) | async-done | bytes 2097184 | tf_op jit(solution)/shard_map/all_to_all | solution.py:40
  76.6 2.7 fusion.99
  79.3 1.7 copy.26
  81.0 1.5 squeeze.9
  82.5 3.3 copy.25
  85.8 2.3 squeeze.8
  88.1 0.6 fusion.100
  89.2 0.9 copy-done.1
  90.1 0.6 fusion.31
  90.8 0.7 fusion.85
  91.8 2.6 collective-permute-done.1
  94.6 20.7 %all_to_all.46 = bf16[8,16,4096]{2,1,0:T(8,128)(2,1)S(1)} all-to-all(bf16[8,16,4096]{2,1,0:T(8,128)(2,1)S(1)} %bitcast.131), channel_id=1, replica_groups=mesh['section'=2,'seq'=8,'mp'=8] {'mp'}, dimensions={0} | all-to-all | bytes 2097152 | tf_op jit(solution)/shard_map/all_to_all | solution.py:54
  116.1 19.3 %all_to_all.47 = bf16[8,16,4096]{2,1,0:T(8,128)(2,1)S(1)} all-to-all(bf16[8,16,4096]{2,1,0:T(8,128)(2,1)S(1)} %broadcast_in_dim.23), channel_id=1, replica_groups=mesh['section'=2,'seq'=8,'mp'=8] {'mp'}, dimensions={0} | all-to-all | bytes 2097152 | tf_op jit(solution)/shard_map/all_to_all | solution.py:40
  135.5 20.3 %all_to_all.48 = bf16[8,16,4096]{2,1,0:T(8,128)(2,1)S(1)} all-to-all(bf16[8,16,4096]{2,1,0:T(8,128)(2,1)S(1)} %stack.12), channel_id=1, replica_groups=mesh['section'=2,'seq'=8,'mp'=8] {'mp'}, dimensions={0} | all-to-all | bytes 2097152 | tf_op jit(solution)/shard_map/all_to_all | solution.py:67
  155.8 6.1 %fusion.7 = f32[256,1024]{1,0:T(8,128)S(1)} fusion(bf16[4096,1024]{1,0:T(8,128)(2,1)} %param.9, bf16[128,4096]{1,0:T(8,128)(2,1)S(1)} %collective-permute-done.2, bf16[128,4096]{1,0:T(8,128)(2,1)S(1)} %bitcast.139), kind=kOutput, calls=%fused_computation.21 | convolution fusion | flops 2151677952 | bytes 11534336 | tf_op jit(solution)/shard_map/dot_general | solution.py:73
  162.0 2.3 fusion.47
  164.3 2.0 copy-done.6
  166.3 1.1 slice.84
  167.4 0.8 collective-permute-start.3
  168.2 13.4 %fusion.45 = f32[256,4096]{1,0:T(8,128)} fusion(bf16[4096,1024]{1,0:T(8,128)(2,1)} %param.9, bf16[1024,4096]{1,0:T(8,128)(2,1)} %param.10, bf16[128,4096]{1,0:T(8,128)(2,1)} %collective-permute-done.4, bf16[128,4096]{1,0:T(8,128)(2,1)} %bitcast.137, f32[256,1024]{1,0:T(8,128)} %copy-done.11), kind=kOutput, calls=%fused_computation.63 | convolution fusion | flops 4301783040 | bytes 24117248 | tf_op jit(solution)/shard_map/tf,df->td/dot_general | solution.py:77
  181.7 2.7 slice.83
  184.4 3.0 fusion.2
  187.5 2.1 fusion.1
  189.5 21.1 %all_to_all.49 = bf16[8,16,4096]{2,1,0:T(8,128)(2,1)S(1)} all-to-all(bf16[8,16,4096]{2,1,0:T(8,128)(2,1)S(1)} %bitcast.132), channel_id=1, replica_groups=mesh['section'=2,'seq'=8,'mp'=8] {'mp'}, dimensions={0} | all-to-all | bytes 2097152 | tf_op jit(solution)/shard_map/all_to_all | solution.py:54
  211.1 47.0 %reduce-scatter.2.cloned.1.call-done = bf16[16,4096]{1,0:T(8,128)(2,1)} async-done(((bf16[128,4096]{1,0:T(8,128)(2,1)}), bf16[16,4096]{1,0:T(8,128)(2,1)}) %reduce-scatter.2.cloned.1.call-update) | async-done | bytes 131088 | tf_op jit(solution)/shard_map/reduce_scatter | solution.py:62
  258.2 1.7 fusion.63
  260.1 19.8 %all_to_all.50 = bf16[8,16,4096]{2,1,0:T(8,128)(2,1)S(1)} all-to-all(bf16[8,16,4096]{2,1,0:T(8,128)(2,1)S(1)} %broadcast_in_dim.26), channel_id=1, replica_groups=mesh['section'=2,'seq'=8,'mp'=8] {'mp'}, dimensions={0} | all-to-all | bytes 2097152 | tf_op jit(solution)/shard_map/all_to_all | solution.py:40
  280.0 2.6 collective-permute-done.6
  282.6 0.7 fusion.32
  283.6 2.3 convolution_convert_fusion
  285.9 2.0 multiply_convert_fusion
  289.3 1.5 maximum_bitcast_fusion.2
  290.8 4.3 %all-to-all-start.7 = ((bf16[8,2,2,128,256]{3,4,2,1,0:T(8,128)(2,1)}), bf16[8,2,2,128,256]{3,4,2,1,0:T(8,128)(2,1)}, u32[]{:S(2)}, u32[]{:S(2)}) async-start(bf16[8,2,2,128,256]{3,4,2,1,0:T(8,128)(2,1)} %maximum_bitcast_fusion.2), calls=%async_computation.8 | async-start | bytes 4194304 | tf_op jit(solution)/shard_map/all_to_all | solution.py:154
  295.1 1.7 fusion.35
  297.0 25.7 %all-to-all-done.7 = bf16[8,2,2,128,256]{3,4,2,1,0:T(8,128)(2,1)} async-done(((bf16[8,2,2,128,256]{3,4,2,1,0:T(8,128)(2,1)}), bf16[8,2,2,128,256]{3,4,2,1,0:T(8,128)(2,1)}, u32[]{:S(2)}, u32[]{:S(2)}) %all-to-all-start.7) | async-done | bytes 2097184 | tf_op jit(solution)/shard_map/all_to_all | solution.py:154
  322.7 1.9 reduce_sum.147
  324.8 4.6 %convolution_bitcast_fusion = f32[256,4096]{1,0:T(8,128)S(1)} fusion(bf16[3,4096,256]{2,1,0:T(8,128)(2,1)} %param.7, bf16[2,256,256]{2,1,0:T(8,128)(2,1)S(1)} %bitcast.135, bf16[1,256,256]{2,1,0:T(8,128)(2,1)S(1)} %reshape.282), kind=kOutput, calls=%fused_computation | convolution fusion | flops 1610809344 | bytes 10878976 | tf_op jit(solution)/shard_map/ktf,kdf->td/dot_general | solution.py:160
  329.6 2.6 collective-permute-done.7
  332.5 20.3 %all_to_all.51 = bf16[8,16,4096]{2,1,0:T(8,128)(2,1)S(1)} all-to-all(bf16[8,16,4096]{2,1,0:T(8,128)(2,1)S(1)} %bitcast.133), channel_id=1, replica_groups=mesh['section'=2,'seq'=8,'mp'=8] {'mp'}, dimensions={0} | all-to-all | bytes 2097152 | tf_op jit(solution)/shard_map/all_to_all | solution.py:54
  353.5 0.8 fusion.75
  (82 shorter events, 6.3 us)
Async XLA Ops:
  7.2 83.7 %copy-start = (bf16[256,4096]{1,0:T(8,128)(2,1)S(1)}, bf16[256,4096]{1,0:T(8,128)(2,1)}, u32[]{:S(2)}) copy-start(bf16[256,4096]{1,0:T(8,128)(2,1)} %param.8) | copy-start | bytes 6291460
  35.4 2.7 collective-permute-start
  44.7 32.0 %all-to-all-start.1 = ((bf16[8,2,2,128,256]{3,4,2,1,0:T(8,128)(2,1)}), bf16[8,2,2,128,256]{3,4,2,1,0:T(8,128)(2,1)}, u32[]{:S(2)}, u32[]{:S(2)}) async-start(bf16[8,2,2,128,256]{3,4,2,1,0:T(8,128)(2,1)} %broadcast_in_dim.21), calls=%async_computation.1 | async-start | bytes 4194304 | tf_op jit(solution)/shard_map/all_to_all | solution.py:40
  49.3 208.9 %reduce-scatter.2.cloned.1.call-start = ((), (), s32[]{:S(2)}) async-start(), calls=%async_computation.10 | async-start | bytes 1179648 | tf_op jit(solution)/shard_map/reduce_scatter | solution.py:62
  49.5 38.6 %copy-start.7 = (bf16[2,128,2,128]{1,3,2,0:T(8,128)(2,1)}, bf16[2,128,2,128]{1,3,2,0:T(8,128)(2,1)S(1)}, u32[]{:S(2)}) copy-start(bf16[2,128,2,128]{1,3,2,0:T(8,128)(2,1)S(1)} %copy.34) | copy-start | bytes 393220
  82.5 5.6 %copy-start.3 = (bf16[2,1024,2,128]{1,3,2,0:T(8,128)(2,1)}, bf16[2,1024,2,128]{1,3,2,0:T(8,128)(2,1)S(1)}, u32[]{:S(2)}) copy-start(bf16[2,1024,2,128]{1,3,2,0:T(8,128)(2,1)S(1)} %squeeze.9) | copy-start | bytes 3145732
  88.1 2.0 copy-start.5
  88.7 1.4 copy-start.1
  91.7 2.7 collective-permute-start.1
  94.6 20.8 %copy-start.4 = (bf16[1,16,4096]{2,1,0:T(8,128)(2,1)S(1)}, bf16[1,16,4096]{2,1,0:T(8,128)(2,1)}, u32[]{:S(2)}) copy-start(bf16[1,16,4096]{2,1,0:T(8,128)(2,1)} %param.6) | copy-start | bytes 393220
  115.6 19.8 %copy-start.10 = (bf16[1,16,4096]{2,1,0:T(8,128)(2,1)S(1)}, bf16[1,16,4096]{2,1,0:T(8,128)(2,1)}, u32[]{:S(2)}) copy-start(bf16[1,16,4096]{2,1,0:T(8,128)(2,1)} %param.11) | copy-start | bytes 393220
  135.4 20.4 %collective-permute-start.2 = (bf16[128,4096]{1,0:T(8,128)(2,1)S(1)}, bf16[128,4096]{1,0:T(8,128)(2,1)S(1)}, u32[]{:S(2)}, u32[]{:S(2)}) collective-permute-start(bf16[128,4096]{1,0:T(8,128)(2,1)S(1)} %bitcast.138), channel_id=1, source_target_pairs={{0,64},{64,0},{1,65},{65,1},{2,66},{66,2},{3,67},{67,3},{4,68},{68... | collective-permute-start | bytes 3145736 | tf_op jit(solution)/shard_map/ppermute | solution.py:34
  155.8 6.2 %copy-start.9 = (bf16[8,16,4096]{2,1,0:T(8,128)(2,1)}, bf16[8,16,4096]{2,1,0:T(8,128)(2,1)S(1)}, u32[]{:S(2)}) copy-start(bf16[8,16,4096]{2,1,0:T(8,128)(2,1)S(1)} %all_to_all.48) | copy-start | bytes 3145732
  155.8 6.2 %slice-start = ((s8[8388608]{0:T(1024)(128)(4,1)}), s8[4194304]{0:T(1024)(128)(4,1)S(1)}, s32[]{:S(2)}) async-start(s8[8388608]{0:T(1024)(128)(4,1)} %bitcast.149), calls=%async_computation.11 | async-start | bytes 8388608
  155.8 6.2 %slice-start.1 = ((s8[8388608]{0:T(1024)(128)(4,1)}), s8[4194304]{0:T(1024)(128)(4,1)S(1)}, s32[]{:S(2)}) async-start(s8[8388608]{0:T(1024)(128)(4,1)} %bitcast.149), calls=%async_computation.12 | async-start | bytes 8388608
  155.8 12.5 %collective-permute-start.4 = (bf16[128,4096]{1,0:T(8,128)(2,1)S(1)}, bf16[128,4096]{1,0:T(8,128)(2,1)}, u32[]{:S(2)}, u32[]{:S(2)}) collective-permute-start(bf16[128,4096]{1,0:T(8,128)(2,1)S(1)} %bitcast.136), channel_id=1, source_target_pairs={{0,64},{64,0},{1,65},{65,1},{2,66},{66,2},{3,67},{67,3},{4,68},{68... | collective-permute-start | bytes 3145736 | tf_op jit(solution)/shard_map/ppermute | solution.py:34
  162.0 2.3 copy-start.11
  164.3 2.0 copy-start.6
  167.4 17.0 %collective-permute-start.3 = (bf16[128,4096]{1,0:T(8,128)(2,1)}, bf16[128,4096]{1,0:T(8,128)(2,1)}, u32[]{:S(2)}, u32[]{:S(2)}) collective-permute-start(bf16[128,4096]{1,0:T(8,128)(2,1)} %slice.84), channel_id=1, source_target_pairs={{0,64},{64,0},{1,65},{65,1},{2,66},{66,2},{3,67},{67,3},{4,68},{68... | collective-permute-start | bytes 3145736 | tf_op jit(solution)/shard_map/ppermute | solution.py:34
  184.4 3.1 collective-permute-start.5
  280.0 2.7 collective-permute-start.6
  283.5 2.3 copy-start.2
  285.9 2.0 copy-start.8
  290.8 31.9 %all-to-all-start.7 = ((bf16[8,2,2,128,256]{3,4,2,1,0:T(8,128)(2,1)}), bf16[8,2,2,128,256]{3,4,2,1,0:T(8,128)(2,1)}, u32[]{:S(2)}, u32[]{:S(2)}) async-start(bf16[8,2,2,128,256]{3,4,2,1,0:T(8,128)(2,1)} %maximum_bitcast_fusion.2), calls=%async_computation.8 | async-start | bytes 4194304 | tf_op jit(solution)/shard_map/all_to_all | solution.py:154
  329.5 2.7 collective-permute-start.7
Sparse Core Ops, SparseCore 0:
  187.6 70.5 reduce-scatter.1
